TPU v7x, 32 devices: a whole 2x2x4 slice. The times are simulated.
32 devices in a mesh: row: 4 (over y, x), col: 2 (over core), depth: 4 (over z).
Axes of the slice: x: 2, y: 2, z: 4, core: 2. Of those that a mesh axis runs over, the one named last changes fastest.
Arguments:
- left_slab: bfloat16 [4096, 4096], P(None, ('col', 'depth')), may hold values from -6 to 6
- right_vectors: bfloat16 [65536, 4096], P('col', 'depth'), may hold values from -0.09375 to 0.09375
- pair_weight: float32 [4096], P(('col', 'depth')), may hold values from -6 to 6
- eigenvalue: float32 [4096], P(('col', 'depth')), may hold values from -2 to 2
- pair_order: int32 [4096], replicated, may hold values from 0 to 4095, each once
- row_offset: int32 [1], replicated, may hold values from 0 to 3072
Outputs:
- grads: bfloat16 [3, 1024, 65536], P(None, 'row', ('col', 'depth'))
Inputs may be any that keep to these rules, and one draw needn't show every extreme that they name: `pair_order`: each of 0 to 4095 appears exactly once.
All inputs are finite; a program needn't handle non-finite values.
Results may differ from a plain program's by a relative error of at most 0.023.
Values may be sent and summed in bfloat16 or wider, within the bound.
A program may use at most 192 MiB of HBM per device.

v0:
```python
import jax
import jax.numpy as jnp
from jax import lax
from jax.sharding import PartitionSpec as P

P_SIZE = 1024


def scale_rows(left, weight, lam, columns):
    picked = jnp.take(left, columns, axis=1).astype(jnp.float32)
    w_pick = jnp.take(weight, columns)
    l_pick = jnp.take(lam, columns)
    powers = jnp.stack([w_pick, w_pick * l_pick, w_pick * l_pick * l_pick])
    scaled = (picked[None, :, :] * powers[:, None, :]).astype(jnp.bfloat16)
    return scaled.reshape(3 * left.shape[0], columns.shape[0])


def on_device(left_slab, right_vectors, pair_weight, eigenvalue, pair_order, row_offset):
    panel_rows = P_SIZE // lax.axis_size("row")
    start = row_offset[0] + lax.axis_index("row") * panel_rows
    local_rows = lax.dynamic_slice_in_dim(left_slab, start, panel_rows, 0)
    pieces = (local_rows, pair_weight[None, :], eigenvalue[None, :])
    left, weight, lam = (
        lax.all_gather(pieces[0], ("col", "depth"), axis=1, tiled=True),
        lax.all_gather(pieces[1].astype(jnp.bfloat16), ("col", "depth"), axis=1, tiled=True).astype(
            jnp.float32
        ),
        lax.all_gather(pieces[2].astype(jnp.bfloat16), ("col", "depth"), axis=1, tiled=True).astype(
            jnp.float32
        ),
    )
    weight = weight[0]
    lam = lam[0]
    group_width = right_vectors.shape[1]
    members = lax.dynamic_slice_in_dim(
        pair_order, lax.axis_index("depth") * group_width, group_width, 0
    )
    scaled = scale_rows(left, weight, lam, members)
    partial_sums = lax.dot_general(
        scaled, right_vectors, (((1,), (1,)), ((), ())), preferred_element_type=jnp.float32
    )
    partial_sums = partial_sums.reshape(3, panel_rows, right_vectors.shape[0])
    total = lax.psum_scatter(
        partial_sums.astype(jnp.bfloat16), "depth", scatter_dimension=2, tiled=True
    )
    return total


def solution(mesh):
    in_specs = (
        P(None, ("col", "depth")),
        P("col", "depth"),
        P(("col", "depth")),
        P(("col", "depth")),
        P(),
        P(),
    )
    out_specs = P(None, "row", ("col", "depth"))
    return jax.shard_map(
        on_device, mesh=mesh, in_specs=in_specs, out_specs=out_specs, check_vma=False
    )
```

profile of v0, /device:TPU:17, one launch (start us, length us, event | category | flops | bytes accessed | tf_op | source)
XLA Modules:
  0.0 962.6 jit_solution(8762134403214115964)
XLA Ops:
  6.5 0.0 all-gather.6.cloned.1.call-start
  7.2 1.0 constant_dynamic-slice_fusion
  8.2 0.8 copy.13
  9.1 0.0 all-gather.6.cloned.1.call-update
  9.1 0.0 reduce-scatter.2.cloned.1.call-start
  9.1 0.7 convert_element_type.30
  9.8 0.7 convert_element_type.32
  10.5 20.0 %all-gather.3 = bf16[8,1,512]{2,1,0:T(2,128)(2,1)S(1)} all-gather(bf16[1,1,512]{2,1,0:T(2,128)(2,1)S(1)} %reshape.73), channel_id=3, replica_groups=mesh['row'=4,'col'=2,'depth'=4] {'col','depth'}, dimensions={0}, use_global_device_ids=true | all-gather | bytes 9216 | tf_op jit(solution)/shard_map/all_gather | solution.py:28
  30.5 20.5 %all-gather.2 = bf16[8,1,512]{2,1,0:T(2,128)(2,1)S(1)} all-gather(bf16[1,1,512]{2,1,0:T(2,128)(2,1)S(1)} %reshape.71), channel_id=2, replica_groups=mesh['row'=4,'col'=2,'depth'=4] {'col','depth'}, dimensions={0}, use_global_device_ids=true | all-gather | bytes 9216 | tf_op jit(solution)/shard_map/all_gather | solution.py:25
  51.0 0.7 fusion.7
  51.7 6.1 gather_fusion.2
  57.8 6.2 gather_fusion.1
  64.0 0.7 broadcast_select_fusion.1
  64.7 0.0 all-gather.6.cloned.1.call-done
  64.8 5.3 gather_fusion
  70.1 0.2 convert_bitcast_fusion
  70.3 0.3 copy.12
  70.6 59.6 %fusion.2 = bf16[3,256,32768]{2,1,0:T(8,128)(2,1)} fusion(bf16[32768,1024]{1,0:T(8,128)(2,1)} %param.9, f32[3,1024]{1,0:T(4,128)S(1)} %pad_maximum_fusion, f32[256,1024]{1,0:T(8,128)S(1)} %copy.12), kind=kOutput, calls=%fused_computation.5 | convolution fusion | flops 51566346240 | bytes 118501376 | tf_op jit(solution)/shard_map/dot_general | solution.py:39
  130.2 0.0 reduce-scatter.2.cloned.1.call-update
  130.3 825.5 %reduce-scatter.2.cloned.1.call-done = bf16[3,256,8192]{2,1,0:T(8,128)(2,1)} async-done(((bf16[3,256,32768]{2,1,0:T(8,128)(2,1)}), bf16[3,256,8192]{2,1,0:T(8,128)(2,1)}) %reduce-scatter.2.cloned.1.call-update) | async-done | bytes 12582928 | tf_op jit(solution)/shard_map/reduce_scatter | solution.py:43
  (6 shorter events, 0.1 us)
Async XLA Ops:
  6.5 58.2 %all-gather.6.cloned.1.call-start = ((), (), s32[]{:S(2)}) async-start(), calls=%async_computation.1 | async-start | bytes 2359296 | tf_op jit(solution)/shard_map/all_gather | solution.py:24
  9.1 946.6 %reduce-scatter.2.cloned.1.call-start = ((), (), s32[]{:S(2)}) async-start(), calls=%async_computation.2 | async-start | bytes 62914560 | tf_op jit(solution)/shard_map/reduce_scatter | solution.py:43
Sparse Core Ops, SparseCore 0:
  9.2 30.2 all-gather.5
  130.4 825.2 reduce-scatter.1
where the time goes:
time: 963 us
  waiting for transfers between devices  826 us (86%)
  matrix products  59.6 us (6%)
  blocking collectives  40.4 us (4%)
  local copies, waits for them, and re-layouts  19.8 us (2%)
  between operations  14.1 us (1%)
    reduce_scatter x1, waiting for transfers between devices, on_device(): lax.psum_scatter(partial_sums.astype(jnp.bfloat16), 'depth', scatter_dime...  825 us
    dot_general x1, matrix products, on_device(): lax.dot_general(scaled, right_vectors, (((1,), (1,)), ((), ())), preferre...  59.6 us
    all_gather x1, blocking collectives, on_device(): lax.all_gather(pieces[1].astype(jnp.bfloat16), ('col', 'depth'), axis=1,...  20.5 us
    all_gather x1, blocking collectives, on_device(): lax.all_gather(pieces[2].astype(jnp.bfloat16), ('col', 'depth'), axis=1,...  20 us
  transfers between devices with their start and end apart: 2, of which 1 were waited for; matrix products, arithmetic and copies ran while one was open for 2% of the time, Pallas kernels for 0%

commit v1 on v0

v1 whole, which is shorter than its diff:
```python
import jax
import jax.numpy as jnp
from jax import lax
from jax.sharding import PartitionSpec as P

P_SIZE = 1024
SCALARS = 16


def split_widths(width):
    if width % 2048 == 0:
        unit = width // 16
        return [4 * unit, 4 * unit, 4 * unit, 2 * unit, 2 * unit]
    return [width]


def two_halves(values):
    high = values.astype(jnp.bfloat16)
    low = (values - high.astype(jnp.float32)).astype(jnp.bfloat16)
    return [high, low]


def gather_panel(left_slab, pair_weight, eigenvalue, members, row_offset):
    rows = P_SIZE // lax.axis_size("row")
    start = row_offset[0] + lax.axis_index("row") * rows
    mine = lax.dynamic_slice_in_dim(left_slab, start, rows, 0)
    scalars = jnp.stack(two_halves(pair_weight) + two_halves(eigenvalue))
    scalars = jnp.pad(scalars, ((0, SCALARS - scalars.shape[0]), (0, 0)))
    block = jnp.concatenate([mine, scalars], axis=0)
    block = lax.all_gather(block, ("col", "depth"), axis=1, tiled=True)
    block = jnp.take(block, members, axis=1)
    scalars = block[rows:].astype(jnp.float32)
    weight = scalars[0] + scalars[1]
    lam = scalars[2] + scalars[3]
    panel = lax.all_gather(block[:rows], "row", axis=0, tiled=False)
    powers = jnp.stack([weight, weight * lam, weight * lam * lam])
    scaled = panel.astype(jnp.float32)[:, None] * powers[None, :, None, :]
    return scaled.astype(jnp.bfloat16).reshape(3 * P_SIZE, members.shape[0])


def on_device(left_slab, right_vectors, pair_weight, eigenvalue, pair_order, row_offset):
    n_row, n_depth = lax.axis_size("row"), lax.axis_size("depth")
    row, depth = lax.axis_index("row"), lax.axis_index("depth")
    group = right_vectors.shape[1]
    owned = right_vectors.shape[0] // n_depth
    quarter = owned // n_row
    rows = P_SIZE // n_row

    sources = lax.rem(depth - jnp.arange(n_depth, dtype=jnp.int32) + n_depth, n_depth)
    members = jnp.take(pair_order.reshape(n_depth, group), sources, axis=0).reshape(-1)

    widths = split_widths(quarter)
    offsets = [sum(widths[:j]) for j in range(len(widths))]
    received = []
    for j, (offset, width) in enumerate(zip(offsets, widths)):
        pieces = []
        for step in range(n_depth):
            target = lax.rem(depth + step, n_depth)
            begin = target * owned + row * quarter + offset
            pieces.append(lax.dynamic_slice(right_vectors, (begin, 0), (width, group)))
        if j >= 2:
            tied = lax.optimization_barrier((pieces[1:], received[j - 2]))
            pieces[1:], received[j - 2] = tied
        for step in range(1, n_depth):
            pieces[step] = lax.ppermute(
                pieces[step], "depth", [(i, (i + step) % n_depth) for i in range(n_depth)]
            )
        received.append(pieces)

    scaled = gather_panel(left_slab, pair_weight, eigenvalue, members, row_offset)

    total = jnp.zeros((3, rows, owned), jnp.bfloat16)
    for offset, width, pieces in zip(offsets, widths, received):
        columns = jnp.concatenate(pieces, axis=1)
        part = lax.dot_general(
            scaled, columns, (((1,), (1,)), ((), ())), preferred_element_type=jnp.float32
        ).astype(jnp.bfloat16)
        part = part.reshape(n_row, 3, rows, width)
        for step in range(n_row):
            other = row ^ step
            piece = lax.dynamic_index_in_dim(part, other, 0, keepdims=False)
            if step:
                piece = lax.ppermute(piece, "row", [(i, i ^ step) for i in range(n_row)])
            total = lax.dynamic_update_slice(total, piece, (0, 0, other * quarter + offset))
    return total


def solution(mesh):
    in_specs = (
        P(None, ("col", "depth")),
        P("col", "depth"),
        P(("col", "depth")),
        P(("col", "depth")),
        P(),
        P(),
    )
    out_specs = P(None, "row", ("col", "depth"))
    return jax.shard_map(
        on_device, mesh=mesh, in_specs=in_specs, out_specs=out_specs, check_vma=False
    )
```

time: 963 us -> 625 us (0.65)
  waiting for transfers between devices: 826 us -> 378 us
  local copies, waits for them, and re-layouts: 19.8 us -> 78.2 us
  blocking collectives: 40.4 us -> 0 us
  starting transfers between devices: 0.04 us -> 32.8 us
  other arithmetic: 3.03 us -> 34.6 us
  matrix products: 59.6 us -> 82.8 us
    reduce_scatter x1 -> x0, waiting for transfers between devices: 825 us -> none  [on_device(): lax.psum_scatter(partial_sums.astype(jnp.bfloat16), 'depth', scatter_dime...]
    ppermute x0 -> x30, waiting for transfers between devices: none -> 341 us  [the longest x15 276 us: on_device(): lax.ppermute(pieces[step], 'depth', [(i, (i + step) % n_depth) for i in r...]
    all_gather x2 -> x0, blocking collectives: 40.4 us -> none  [the longest x1 20.5 us: on_device(): lax.all_gather(pieces[1].astype(jnp.bfloat16), ('col', 'depth'), axis=1,...]
    all_gather x1 -> x2, waiting for transfers between devices: 0.02 us -> 37.3 us  [the longest x1 37.3 us: gather_panel(): block = lax.all_gather(block, ('col', 'depth'), axis=1, tiled=True)]
    ppermute x0 -> x30, starting transfers between devices: none -> 32.7 us  [the longest x15 17 us: on_device(): lax.ppermute(pieces[step], 'depth', [(i, (i + step) % n_depth) for i in r...]
    convert_element_type x3 -> x5, other arithmetic: 1.57 us -> 31.7 us  [the longest x1 18.7 us: gather_panel(): return scaled.astype(jnp.bfloat16).reshape(3 * P_SIZE, members.shape[0])]
    dynamic_update_slice x0 -> x20, local copies, waits for them, and re-layouts: none -> 26.2 us  [on_device(): lax.dynamic_update_slice(total, piece, (0, 0, other * quarter + offset))]
    dot_general x1 -> x5, matrix products: 59.6 us -> 82.8 us  [on_device(): lax.dot_general(scaled, columns, (((1,), (1,)), ((), ())), preferred_elem...]
  transfers between devices with their start and end apart: 2 -> 32, of which waited for: 1 -> 15; matrix products, arithmetic and copies ran while one was open for 2% -> 27% of each run, Pallas kernels for 0% -> 0%
where the time goes in v1:
time: 625 us; the launch traced here: 621 us
  waiting for transfers between devices  378 us (60%)
  matrix products  82.8 us (13%)
  local copies, waits for them, and re-layouts  78.2 us (13%)
  other arithmetic  34.6 us (6%)
  starting transfers between devices  32.8 us (5%)
  between operations  14.4 us (2%)
    ppermute x15, waiting for transfers between devices, on_device(): lax.ppermute(pieces[step], 'depth', [(i, (i + step) % n_depth) for i in r...  276 us
    dot_general x5, matrix products, on_device(): lax.dot_general(scaled, columns, (((1,), (1,)), ((), ())), preferred_elem...  82.8 us
    ppermute x15, waiting for transfers between devices, on_device(): piece = lax.ppermute(piece, 'row', [(i, i ^ step) for i in range(n_row)])  65 us
    all_gather x1, waiting for transfers between devices, gather_panel(): block = lax.all_gather(block, ('col', 'depth'), axis=1, tiled=True)  37.3 us
    dynamic_update_slice x20, local copies, waits for them, and re-layouts, on_device(): lax.dynamic_update_slice(total, piece, (0, 0, other * quarter + offset))  26.2 us
    gather x2, local copies, waits for them, and re-layouts, gather_panel(): block = jnp.take(block, members, axis=1)  19 us
    convert_element_type x1, other arithmetic, gather_panel(): return scaled.astype(jnp.bfloat16).reshape(3 * P_SIZE, members.shape[0])  18.7 us
    ppermute x15, starting transfers between devices, on_device(): lax.ppermute(pieces[step], 'depth', [(i, (i + step) % n_depth) for i in r...  17 us
  transfers between devices with their start and end apart: 32, of which 15 were waited for; matrix products, arithmetic and copies ran while one was open for 27% of the time, Pallas kernels for 0%

profile of v1, /device:TPU:17, one launch (start us, length us, event | category | flops | bytes accessed | tf_op | source)
XLA Modules:
  0.0 621.3 jit_solution(15873257217749616081)
XLA Ops:
  12.5 37.3 %all-gather.4.cloned.1.call-done = bf16[272,4096]{0,1:T(8,128)(2,1)} async-done(((bf16[272,512]{0,1:T(8,128)(2,1)}), bf16[272,4096]{0,1:T(8,128)(2,1)}) %all-gather.4.cloned.1.call-update) | async-done | bytes 2228240 | tf_op jit(solution)/shard_map/all_gather | solution.py:30
  49.8 16.3 %gather_fusion.1 = bf16[4096,272]{1,0:T(8,128)(2,1)S(1)} fusion(bf16[272,4096]{0,1:T(8,128)(2,1)} %all-gather.4.cloned.1.call-done, s32[4096]{0:T(1024)S(1)} %broadcast_clamp_fusion), kind=kCustom, calls=%fused_computation.1 | custom fusion | bytes 4472832 | tf_op jit(solution)/shard_map/jit(_take)/gather | solution.py:31
  72.1 8.1 %constant_dynamic-slice_fusion.2 = (bf16[512,1024]{1,0:T(8,128)(2,1)}, bf16[512,1024]{1,0:T(8,128)(2,1)S(1)}, bf16[512,1024]{1,0:T(8,128)(2,1)}, bf16[512,1024]{...) fusion(bf16[32768,1024]{1,0:T(8,128)(2,1)} %param.7, ...), kind=kLoop, calls=%fused_computation.85 | loop fusion | bytes 25165872 | tf_op jit(solution)/shard_map/dynamic_slice | solution.py:60
  86.3 18.5 %collective-permute-done.2 = bf16[512,1024]{1,0:T(8,128)(2,1)S(1)} collective-permute-done((bf16[512,1024]{1,0:T(8,128)(2,1)S(1)}, bf16[512,1024]{1,0:T(8,128)(2,1)S(1)}, u32[]{:S(2)}, u32[]{:S(2)}) %collective-permute-start.2) | collective-permute-done | bytes 1048608 | tf_op jit(solution)/shard_map/ppermute | solution.py:65
  107.0 63.5 %collective-permute-done.1 = bf16[512,1024]{1,0:T(8,128)(2,1)S(1)} collective-permute-done((bf16[512,1024]{1,0:T(8,128)(2,1)S(1)}, bf16[512,1024]{1,0:T(8,128)(2,1)S(1)}, u32[]{:S(2)}, u32[]{:S(2)}) %collective-permute-start.1) | collective-permute-done | bytes 1048608 | tf_op jit(solution)/shard_map/ppermute | solution.py:65
  170.4 48.3 %collective-permute-done = bf16[512,1024]{1,0:T(8,128)(2,1)S(1)} collective-permute-done((bf16[512,1024]{1,0:T(8,128)(2,1)S(1)}, bf16[512,1024]{1,0:T(8,128)(2,1)S(1)}, u32[]{:S(2)}, u32[]{:S(2)}) %collective-permute-start) | collective-permute-done | bytes 1048608 | tf_op jit(solution)/shard_map/ppermute | solution.py:65
  219.2 63.6 %collective-permute-done.8 = bf16[512,1024]{1,0:T(8,128)(2,1)S(1)} collective-permute-done((bf16[512,1024]{1,0:T(8,128)(2,1)S(1)}, bf16[512,1024]{1,0:T(8,128)(2,1)S(1)}, u32[]{:S(2)}, u32[]{:S(2)}) %collective-permute-start.8) | collective-permute-done | bytes 1048608 | tf_op jit(solution)/shard_map/ppermute | solution.py:65
  290.1 15.3 %collective-permute-done.7 = bf16[512,1024]{1,0:T(8,128)(2,1)} collective-permute-done((bf16[512,1024]{1,0:T(8,128)(2,1)}, bf16[512,1024]{1,0:T(8,128)(2,1)}, u32[]{:S(2)}, u32[]{:S(2)}) %collective-permute-start.7) | collective-permute-done | bytes 1048608 | tf_op jit(solution)/shard_map/ppermute | solution.py:65
  309.2 44.5 %collective-permute-done.12 = bf16[512,1024]{1,0:T(8,128)(2,1)} collective-permute-done((bf16[512,1024]{1,0:T(8,128)(2,1)}, bf16[512,1024]{1,0:T(8,128)(2,1)}, u32[]{:S(2)}, u32[]{:S(2)}) %collective-permute-start.12) | collective-permute-done | bytes 1048608 | tf_op jit(solution)/shard_map/ppermute | solution.py:65
  353.7 19.2 %collective-permute-done.14 = bf16[512,1024]{1,0:T(8,128)(2,1)} collective-permute-done((bf16[512,1024]{1,0:T(8,128)(2,1)}, bf16[512,1024]{1,0:T(8,128)(2,1)}, u32[]{:S(2)}, u32[]{:S(2)}) %collective-permute-start.14) | collective-permute-done | bytes 1048608 | tf_op jit(solution)/shard_map/ppermute | solution.py:65
  372.9 4.5 collective-permute-start.24
  377.5 11.4 %convert = f32[4,256,4096]{2,1,0:T(8,128)} convert(bf16[4,256,4096]{2,1,0:T(8,128)(2,1)} %bitcast.76) | non-fusion elementwise | flops 4194304 | bytes 25165824 | tf_op jit(solution)/shard_map/convert_element_type | solution.py:37
  388.9 18.7 %multiply_convert_fusion = bf16[4,3,256,4096]{3,2,1,0:T(8,128)(2,1)} fusion(f32[3,4096]{1,0:T(4,128)S(1)} %pad_maximum_fusion, f32[4,256,4096]{2,1,0:T(8,128)} %convert), kind=kLoop, calls=%fused_computation.2 | loop fusion | flops 25165824 | bytes 41992192 | tf_op jit(solution)/shard_map/convert_element_type | solution.py:38
  407.7 20.2 %convolution_convert_fusion.1 = bf16[3072,512]{1,0:T(8,128)(2,1)} fusion(bf16[3072,4096]{1,0:T(8,128)(2,1)} %bitcast.71, bf16[512,1024]{1,0:T(8,128)(2,1)} %copy-done.14, bf16[512,1024]{1,0:T(8,128)(2,1)} %collective-permute-done.7, bf16[512,1024]{1,0:T(8,128)(2,1)} %collective-permute-done.6, bf16[512,1024]{1,0:T(8,128)(2,1)S(1)} %copy-done.3), kind=kOutput, calls=%fused_computation.4 | convolution fusion | flops 12903251968 | bytes 32505856 | tf_op jit(solution)/shard_map/dot_general | solution.py:75
  427.9 20.0 %convolution_convert_fusion.2 = bf16[3072,512]{1,0:T(8,128)(2,1)} fusion(bf16[3072,4096]{1,0:T(8,128)(2,1)} %bitcast.72, bf16[512,1024]{1,0:T(8,128)(2,1)S(1)} %copy-done.11, bf16[512,1024]{1,0:T(8,128)(2,1)} %copy-done.12, bf16[512,1024]{1,0:T(8,128)(2,1)} %copy-done.13, bf16[512,1024]{1,0:T(8,128)(2,1)S(1)} %get-tuple-element.26), kind=kOutput, calls=%fused_computation.5 | convolution fusion | flops 12903251968 | bytes 32505856 | tf_op jit(solution)/shard_map/dot_general | solution.py:75
  447.8 18.1 %convolution_convert_fusion = bf16[3072,512]{1,0:T(8,128)(2,1)S(1)} fusion(bf16[3072,4096]{1,0:T(8,128)(2,1)} %bitcast.73, bf16[512,1024]{1,0:T(8,128)(2,1)} %collective-permute-done.14, bf16[512,1024]{1,0:T(8,128)(2,1)} %collective-permute-done.13, bf16[512,1024]{1,0:T(8,128)(2,1)} %collective-permute-done.12, bf16[512,1024]{1,0:T(8,128)(2,1)} %get-tuple-element.37), kind=kOutput, calls=%fused_computation.3 | convolution fusion | flops 12903251968 | bytes 32505856 | tf_op jit(solution)/shard_map/dot_general | solution.py:75
  472.5 12.5 %convolution_convert_fusion.4 = bf16[3072,256]{1,0:T(8,128)(2,1)S(1)} fusion(bf16[3072,4096]{1,0:T(8,128)(2,1)} %bitcast.74, bf16[256,1024]{1,0:T(8,128)(2,1)} %collective-permute-done.20, bf16[256,1024]{1,0:T(8,128)(2,1)} %collective-permute-done.19, bf16[256,1024]{1,0:T(8,128)(2,1)} %collective-permute-done.18, bf16[256,1024]{1,0:T(8,128)(2,1)} %get-tuple-element.61), kind=kOutput, calls=%fused_computation.28 | convolution fusion | flops 6451625984 | bytes 28835840 | tf_op jit(solution)/shard_map/dot_general | solution.py:75
  489.2 12.0 %convolution_convert_fusion.3 = bf16[3072,256]{1,0:T(8,128)(2,1)S(1)} fusion(bf16[3072,4096]{1,0:T(8,128)(2,1)} %bitcast.75, bf16[256,1024]{1,0:T(8,128)(2,1)S(1)} %collective-permute-done.26, bf16[256,1024]{1,0:T(8,128)(2,1)} %collective-permute-done.25, bf16[256,1024]{1,0:T(8,128)(2,1)} %collective-permute-done.24, bf16[256,1024]{1,0:T(8,128)(2,1)S(1)} %copy-done.4), kind=kOutput, calls=%fused_computation.27 | convolution fusion | flops 6451625984 | bytes 28835840 | tf_op jit(solution)/shard_map/dot_general | solution.py:75
  505.9 6.3 %broadcast_in_dim.25 = bf16[3,256,8192]{2,1,0:T(8,128)(2,1)} broadcast(bf16[]{:T(256)} %constant.133.clone.1), dimensions={} | broadcast | bytes 12582914 | tf_op jit(solution)/shard_map/broadcast_in_dim | solution.py:72
  530.7 9.1 %collective-permute-done.11 = bf16[3,256,512]{2,1,0:T(8,128)(2,1)S(1)} collective-permute-done((bf16[3,256,512]{2,1,0:T(8,128)(2,1)}, bf16[3,256,512]{2,1,0:T(8,128)(2,1)S(1)}, u32[]{:S(2)}, u32[]{:S(2)}) %collective-permute-start.11) | collective-permute-done | bytes 786464 | tf_op jit(solution)/shard_map/ppermute | solution.py:83
  543.3 13.8 %collective-permute-done.15 = bf16[3,256,512]{2,1,0:T(8,128)(2,1)S(1)} collective-permute-done((bf16[3,256,512]{2,1,0:T(8,128)(2,1)}, bf16[3,256,512]{2,1,0:T(8,128)(2,1)S(1)}, u32[]{:S(2)}, u32[]{:S(2)}) %collective-permute-start.15) | collective-permute-done | bytes 786464 | tf_op jit(solution)/shard_map/ppermute | solution.py:83
  561.3 12.3 %collective-permute-done.17 = bf16[3,256,512]{2,1,0:T(8,128)(2,1)S(1)} collective-permute-done((bf16[3,256,512]{2,1,0:T(8,128)(2,1)}, bf16[3,256,512]{2,1,0:T(8,128)(2,1)S(1)}, u32[]{:S(2)}, u32[]{:S(2)}) %collective-permute-start.17) | collective-permute-done | bytes 786464 | tf_op jit(solution)/shard_map/ppermute | solution.py:83
  578.4 12.5 %collective-permute-done.21 = bf16[3,256,256]{2,1,0:T(8,128)(2,1)S(1)} collective-permute-done((bf16[3,256,256]{2,1,0:T(8,128)(2,1)S(1)}, bf16[3,256,256]{2,1,0:T(8,128)(2,1)S(1)}, u32[]{:S(2)}, u32[]{:S(2)}) %collective-permute-start.21) | collective-permute-done | bytes 393248 | tf_op jit(solution)/shard_map/ppermute | solution.py:83
  592.4 16.4 %collective-permute-done.22 = bf16[3,256,256]{2,1,0:T(8,128)(2,1)S(1)} collective-permute-done((bf16[3,256,256]{2,1,0:T(8,128)(2,1)S(1)}, bf16[3,256,256]{2,1,0:T(8,128)(2,1)S(1)}, u32[]{:S(2)}, u32[]{:S(2)}) %collective-permute-start.22) | collective-permute-done | bytes 393248 | tf_op jit(solution)/shard_map/ppermute | solution.py:83
  (135 shorter events, 84.5 us)
Async XLA Ops:
  6.5 43.2 %all-gather.4.cloned.1.call-start = ((), (), s32[]{:S(2)}) async-start(), calls=%async_computation | async-start | bytes 3538944 | tf_op jit(solution)/shard_map/all_gather | solution.py:30
  10.9 366.6 %all-gather.6.cloned.1.call-start = ((), (), s32[]{:S(2)}) async-start(), calls=%async_computation.1 | async-start | bytes 10485760 | tf_op jit(solution)/shard_map/all_gather | solution.py:35
  80.7 89.8 %collective-permute-start.1 = (bf16[512,1024]{1,0:T(8,128)(2,1)S(1)}, bf16[512,1024]{1,0:T(8,128)(2,1)S(1)}, u32[]{:S(2)}, u32[]{:S(2)}) collective-permute-start(bf16[512,1024]{1,0:T(8,128)(2,1)S(1)} %get-tuple-element.68), channel_id=1, source_target_pairs={{0,2},{1,3},{2,0},{3,1},{4,6},{5,7},{6,4},{7,5},{8,10},{9,11},{10,... | collective-permute-start | bytes 3145736 | tf_op jit(solution)/shard_map/ppermute | solution.py:65
  82.7 136.1 %collective-permute-start = (bf16[512,1024]{1,0:T(8,128)(2,1)S(1)}, bf16[512,1024]{1,0:T(8,128)(2,1)S(1)}, u32[]{:S(2)}, u32[]{:S(2)}) collective-permute-start(bf16[512,1024]{1,0:T(8,128)(2,1)S(1)} %get-tuple-element.69), channel_id=1, source_target_pairs={{0,1},{1,2},{2,3},{3,0},{4,5},{5,6},{6,7},{7,4},{8,9},{9,10},{10,1... | collective-permute-start | bytes 3145736 | tf_op jit(solution)/shard_map/ppermute | solution.py:65
  83.3 199.5 %collective-permute-start.8 = (bf16[512,1024]{1,0:T(8,128)(2,1)S(1)}, bf16[512,1024]{1,0:T(8,128)(2,1)S(1)}, u32[]{:S(2)}, u32[]{:S(2)}) collective-permute-start(bf16[512,1024]{1,0:T(8,128)(2,1)S(1)} %get-tuple-element.63), channel_id=1, source_target_pairs={{0,3},{1,0},{2,1},{3,2},{4,7},{5,4},{6,5},{7,6},{8,11},{9,8},{10,9... | collective-permute-start | bytes 3145736 | tf_op jit(solution)/shard_map/ppermute | solution.py:65
  84.1 221.3 %collective-permute-start.7 = (bf16[512,1024]{1,0:T(8,128)(2,1)}, bf16[512,1024]{1,0:T(8,128)(2,1)}, u32[]{:S(2)}, u32[]{:S(2)}) collective-permute-start(bf16[512,1024]{1,0:T(8,128)(2,1)} %get-tuple-element.64), channel_id=1, source_target_pairs={{0,2},{1,3},{2,0},{3,1},{4,6},{5,7},{6,4},{7,5},{8,10},{9,11},{10,... | collective-permute-start | bytes 3145736 | tf_op jit(solution)/shard_map/ppermute | solution.py:65
  104.8 203.9 %collective-permute-start.6 = (bf16[512,1024]{1,0:T(8,128)(2,1)}, bf16[512,1024]{1,0:T(8,128)(2,1)}, u32[]{:S(2)}, u32[]{:S(2)}) collective-permute-start(bf16[512,1024]{1,0:T(8,128)(2,1)} %get-tuple-element.65), channel_id=1, source_target_pairs={{0,1},{1,2},{2,3},{3,0},{4,5},{5,6},{6,7},{7,4},{8,9},{9,10},{10,1... | collective-permute-start | bytes 3145736 | tf_op jit(solution)/shard_map/ppermute | solution.py:65
  218.7 135.0 %collective-permute-start.12 = (bf16[512,1024]{1,0:T(8,128)(2,1)}, bf16[512,1024]{1,0:T(8,128)(2,1)}, u32[]{:S(2)}, u32[]{:S(2)}) collective-permute-start(bf16[512,1024]{1,0:T(8,128)(2,1)} %get-tuple-element.34), channel_id=1, source_target_pairs={{0,1},{1,2},{2,3},{3,0},{4,5},{5,6},{6,7},{7,4},{8,9},{9,10},{10,1... | collective-permute-start | bytes 3145736 | tf_op jit(solution)/shard_map/ppermute | solution.py:65
  218.7 135.0 %collective-permute-start.13 = (bf16[512,1024]{1,0:T(8,128)(2,1)}, bf16[512,1024]{1,0:T(8,128)(2,1)}, u32[]{:S(2)}, u32[]{:S(2)}) collective-permute-start(bf16[512,1024]{1,0:T(8,128)(2,1)} %get-tuple-element.35), channel_id=1, source_target_pairs={{0,2},{1,3},{2,0},{3,1},{4,6},{5,7},{6,4},{7,5},{8,10},{9,11},{10,... | collective-permute-start | bytes 3145736 | tf_op jit(solution)/shard_map/ppermute | solution.py:65
  283.8 89.1 %collective-permute-start.14 = (bf16[512,1024]{1,0:T(8,128)(2,1)}, bf16[512,1024]{1,0:T(8,128)(2,1)}, u32[]{:S(2)}, u32[]{:S(2)}) collective-permute-start(bf16[512,1024]{1,0:T(8,128)(2,1)} %get-tuple-element.36), channel_id=1, source_target_pairs={{0,3},{1,0},{2,1},{3,2},{4,7},{5,4},{6,5},{7,6},{8,11},{9,8},{10,9... | collective-permute-start | bytes 3145736 | tf_op jit(solution)/shard_map/ppermute | solution.py:65
  308.8 160.3 %collective-permute-start.18 = (bf16[256,1024]{1,0:T(8,128)(2,1)}, bf16[256,1024]{1,0:T(8,128)(2,1)}, u32[]{:S(2)}, u32[]{:S(2)}) collective-permute-start(bf16[256,1024]{1,0:T(8,128)(2,1)} %get-tuple-element.41), channel_id=1, source_target_pairs={{0,1},{1,2},{2,3},{3,0},{4,5},{5,6},{6,7},{7,4},{8,9},{9,10},{10,1... | collective-permute-start | bytes 1572872 | tf_op jit(solution)/shard_map/ppermute | solution.py:65
  308.8 161.5 %collective-permute-start.19 = (bf16[256,1024]{1,0:T(8,128)(2,1)}, bf16[256,1024]{1,0:T(8,128)(2,1)}, u32[]{:S(2)}, u32[]{:S(2)}) collective-permute-start(bf16[256,1024]{1,0:T(8,128)(2,1)} %get-tuple-element.42), channel_id=1, source_target_pairs={{0,2},{1,3},{2,0},{3,1},{4,6},{5,7},{6,4},{7,5},{8,10},{9,11},{10,... | collective-permute-start | bytes 1572872 | tf_op jit(solution)/shard_map/ppermute | solution.py:65
  353.7 118.6 %collective-permute-start.20 = (bf16[256,1024]{1,0:T(8,128)(2,1)}, bf16[256,1024]{1,0:T(8,128)(2,1)}, u32[]{:S(2)}, u32[]{:S(2)}) collective-permute-start(bf16[256,1024]{1,0:T(8,128)(2,1)} %get-tuple-element.43), channel_id=1, source_target_pairs={{0,3},{1,0},{2,1},{3,2},{4,7},{5,4},{6,5},{7,6},{8,11},{9,8},{10,9... | collective-permute-start | bytes 1572872 | tf_op jit(solution)/shard_map/ppermute | solution.py:65
  372.9 113.8 %collective-permute-start.24 = (bf16[256,1024]{1,0:T(8,128)(2,1)}, bf16[256,1024]{1,0:T(8,128)(2,1)}, u32[]{:S(2)}, u32[]{:S(2)}) collective-permute-start(bf16[256,1024]{1,0:T(8,128)(2,1)} %get-tuple-element.44), channel_id=1, source_target_pairs={{0,1},{1,2},{2,3},{3,0},{4,5},{5,6},{6,7},{7,4},{8,9},{9,10},{10,1... | collective-permute-start | bytes 1572872 | tf_op jit(solution)/shard_map/ppermute | solution.py:65
  377.4 109.7 %collective-permute-start.25 = (bf16[256,1024]{1,0:T(8,128)(2,1)}, bf16[256,1024]{1,0:T(8,128)(2,1)}, u32[]{:S(2)}, u32[]{:S(2)}) collective-permute-start(bf16[256,1024]{1,0:T(8,128)(2,1)} %get-tuple-element.45), channel_id=1, source_target_pairs={{0,2},{1,3},{2,0},{3,1},{4,6},{5,7},{6,4},{7,5},{8,10},{9,11},{10,... | collective-permute-start | bytes 1572872 | tf_op jit(solution)/shard_map/ppermute | solution.py:65
  470.2 49.8 %collective-permute-start.5 = (bf16[3,256,512]{2,1,0:T(8,128)(2,1)}, bf16[3,256,512]{2,1,0:T(8,128)(2,1)}, u32[]{:S(2)}, u32[]{:S(2)}) collective-permute-start(bf16[3,256,512]{2,1,0:T(8,128)(2,1)} %get-tuple-element.80), channel_id=1, source_target_pairs={{0,24},{8,16},{16,8},{24,0},{1,25},{9,17},{17,9},{25,1},{2,26},{10... | collective-permute-start | bytes 2359304 | tf_op jit(solution)/shard_map/ppermute | solution.py:83
  472.3 44.7 %collective-permute-start.4 = (bf16[3,256,512]{2,1,0:T(8,128)(2,1)}, bf16[3,256,512]{2,1,0:T(8,128)(2,1)}, u32[]{:S(2)}, u32[]{:S(2)}) collective-permute-start(bf16[3,256,512]{2,1,0:T(8,128)(2,1)} %get-tuple-element.81), channel_id=1, source_target_pairs={{0,16},{8,24},{16,0},{24,8},{1,17},{9,25},{17,1},{25,9},{2,18},{10... | collective-permute-start | bytes 2359304 | tf_op jit(solution)/shard_map/ppermute | solution.py:83
  487.0 39.7 %collective-permute-start.10 = (bf16[3,256,512]{2,1,0:T(8,128)(2,1)}, bf16[3,256,512]{2,1,0:T(8,128)(2,1)}, u32[]{:S(2)}, u32[]{:S(2)}) collective-permute-start(bf16[3,256,512]{2,1,0:T(8,128)(2,1)} %get-tuple-element.78), channel_id=1, source_target_pairs={{0,16},{8,24},{16,0},{24,8},{1,17},{9,25},{17,1},{25,9},{2,18},{10... | collective-permute-start | bytes 2359304 | tf_op jit(solution)/shard_map/ppermute | solution.py:83
  517.0 42.8 %collective-permute-start.16 = (bf16[3,256,512]{2,1,0:T(8,128)(2,1)}, bf16[3,256,512]{2,1,0:T(8,128)(2,1)S(1)}, u32[]{:S(2)}, u32[]{:S(2)}) collective-permute-start(bf16[3,256,512]{2,1,0:T(8,128)(2,1)} %get-tuple-element.75), channel_id=1, source_target_pairs={{0,16},{8,24},{16,0},{24,8},{1,17},{9,25},{17,1},{25,9},{2,18},{10... | collective-permute-start | bytes 2359304 | tf_op jit(solution)/shard_map/ppermute | solution.py:83
  520.1 37.1 %collective-permute-start.15 = (bf16[3,256,512]{2,1,0:T(8,128)(2,1)}, bf16[3,256,512]{2,1,0:T(8,128)(2,1)S(1)}, u32[]{:S(2)}, u32[]{:S(2)}) collective-permute-start(bf16[3,256,512]{2,1,0:T(8,128)(2,1)} %get-tuple-element.76), channel_id=1, source_target_pairs={{0,8},{8,0},{16,24},{24,16},{1,9},{9,1},{17,25},{25,17},{2,10},{10... | collective-permute-start | bytes 2359304 | tf_op jit(solution)/shard_map/ppermute | solution.py:83
  524.2 49.4 %collective-permute-start.17 = (bf16[3,256,512]{2,1,0:T(8,128)(2,1)}, bf16[3,256,512]{2,1,0:T(8,128)(2,1)S(1)}, u32[]{:S(2)}, u32[]{:S(2)}) collective-permute-start(bf16[3,256,512]{2,1,0:T(8,128)(2,1)} %get-tuple-element.74), channel_id=1, source_target_pairs={{0,24},{8,16},{16,8},{24,0},{1,25},{9,17},{17,9},{25,1},{2,26},{10... | collective-permute-start | bytes 2359304 | tf_op jit(solution)/shard_map/ppermute | solution.py:83
  526.7 86.9 %collective-permute-start.29 = (bf16[3,256,256]{2,1,0:T(8,128)(2,1)S(1)}, bf16[3,256,256]{2,1,0:T(8,128)(2,1)S(1)}, u32[]{:S(2)}, u32[]{:S(2)}) collective-permute-start(bf16[3,256,256]{2,1,0:T(8,128)(2,1)S(1)} %get-tuple-element.83), channel_id=1, source_target_pairs={{0,24},{8,16},{16,8},{24,0},{1,25},{9,17},{17,9},{25,1},{2,26},{10... | collective-permute-start | bytes 1179656 | tf_op jit(solution)/shard_map/ppermute | solution.py:83
  539.9 73.0 %collective-permute-start.28 = (bf16[3,256,256]{2,1,0:T(8,128)(2,1)S(1)}, bf16[3,256,256]{2,1,0:T(8,128)(2,1)S(1)}, u32[]{:S(2)}, u32[]{:S(2)}) collective-permute-start(bf16[3,256,256]{2,1,0:T(8,128)(2,1)S(1)} %copy-done.5), channel_id=1, source_target_pairs={{0,16},{8,24},{16,0},{24,8},{1,17},{9,25},{17,1},{25,9},{2,18},{10... | collective-permute-start | bytes 1179656 | tf_op jit(solution)/shard_map/ppermute | solution.py:83
  559.7 49.1 %collective-permute-start.22 = (bf16[3,256,256]{2,1,0:T(8,128)(2,1)S(1)}, bf16[3,256,256]{2,1,0:T(8,128)(2,1)S(1)}, u32[]{:S(2)}, u32[]{:S(2)}) collective-permute-start(bf16[3,256,256]{2,1,0:T(8,128)(2,1)S(1)} %copy-done.8), channel_id=1, source_target_pairs={{0,16},{8,24},{16,0},{24,8},{1,17},{9,25},{17,1},{25,9},{2,18},{10... | collective-permute-start | bytes 1179656 | tf_op jit(solution)/shard_map/ppermute | solution.py:83
  (23 other events, 923.7 us)
Sparse Core Ops, SparseCore 0:
  11.0 38.6 all-gather.3
  72.2 87.1 all-gather.5

commit v2 on v1

v2 whole, which is shorter than its diff:
```python
import jax
import jax.numpy as jnp
from jax import lax
from jax.sharding import PartitionSpec as P

P_SIZE = 1024
SCALARS = 16


def split_widths(width):
    if width % 2048 == 0:
        unit = width // 16
        return [unit, 3 * unit, 5 * unit, 4 * unit, 3 * unit]
    return [width]


def after(values, *earlier):
    return lax.optimization_barrier((values, earlier))[0]


def two_halves(values):
    high = values.astype(jnp.bfloat16)
    low = (values - high.astype(jnp.float32)).astype(jnp.bfloat16)
    return [high, low]


def gather_panel(left_slab, pair_weight, eigenvalue, members, row_offset, arrived):
    rows = P_SIZE // lax.axis_size("row")
    start = row_offset[0] + lax.axis_index("row") * rows
    mine = lax.dynamic_slice_in_dim(left_slab, start, rows, 0)
    scalars = jnp.stack(two_halves(pair_weight) + two_halves(eigenvalue))
    scalars = jnp.pad(scalars, ((0, SCALARS - scalars.shape[0]), (0, 0)))
    block = jnp.concatenate([mine, scalars], axis=0)
    block = after(block, arrived[0])
    block = lax.all_gather(block, ("col", "depth"), axis=1, tiled=True)
    block = jnp.take(block, members, axis=1)
    scalars = block[rows:].astype(jnp.float32)
    weight = scalars[0] + scalars[1]
    lam = scalars[2] + scalars[3]
    panel = block[:rows]
    if len(arrived) > 1:
        panel = after(panel, arrived[1])
    panel = lax.all_gather(panel, "row", axis=0, tiled=False)
    if len(arrived) > 2:
        panel = after(panel, arrived[2])
    powers = jnp.stack([weight, weight * lam, weight * lam * lam])
    scaled = panel.astype(jnp.float32)[:, None] * powers[None, :, None, :]
    return scaled.astype(jnp.bfloat16).reshape(3 * P_SIZE, members.shape[0])


def on_device(left_slab, right_vectors, pair_weight, eigenvalue, pair_order, row_offset):
    n_row, n_depth = lax.axis_size("row"), lax.axis_size("depth")
    row, depth = lax.axis_index("row"), lax.axis_index("depth")
    group = right_vectors.shape[1]
    owned = right_vectors.shape[0] // n_depth
    quarter = owned // n_row
    rows = P_SIZE // n_row

    sources = lax.rem(depth - jnp.arange(n_depth, dtype=jnp.int32) + n_depth, n_depth)
    members = jnp.take(pair_order.reshape(n_depth, group), sources, axis=0).reshape(-1)

    widths = split_widths(quarter)
    offsets = [sum(widths[:j]) for j in range(len(widths))]
    starts = [
        lax.rem(depth + step, n_depth) * owned + row * quarter for step in range(n_depth)
    ]
    received = []
    products = []
    landed = []
    scaled = None

    def fetch(j):
        pieces = [
            lax.dynamic_slice(right_vectors, (begin + offsets[j], 0), (widths[j], group))
            for begin in starts
        ]
        if j >= 2:
            pieces[1:] = after(pieces[1:], received[j - 2][1:])
        if j >= 4:
            pieces[1:] = after(pieces[1:], products[j - 4])
        for step in range(1, n_depth):
            pieces[step] = lax.ppermute(
                pieces[step], "depth", [(i, (i + step) % n_depth) for i in range(n_depth)]
            )
        received.append(pieces)

    def multiply(j):
        pieces = received[j]
        if j >= 1:
            pieces = after(pieces, products[j - 1])
        if j >= 4:
            pieces = after(pieces, landed[j - 2])
        columns = jnp.concatenate(pieces, axis=1)
        part = lax.dot_general(
            scaled, columns, (((1,), (1,)), ((), ())), preferred_element_type=jnp.float32
        ).astype(jnp.bfloat16)
        part = part.reshape(n_row, 3, rows, widths[j])
        products.append(part)
        blocks = []
        for step in range(n_row):
            piece = lax.dynamic_index_in_dim(part, row ^ step, 0, keepdims=False)
            if step:
                piece = lax.ppermute(piece, "row", [(i, i ^ step) for i in range(n_row)])
            blocks.append(piece)
        landed.append(blocks)

    count = len(widths)
    for j in range(min(count, 4)):
        fetch(j)
    scaled = gather_panel(
        left_slab, pair_weight, eigenvalue, members, row_offset, [p[1:] for p in received[:3]]
    )
    for j in range(count):
        multiply(j)
        if j + 4 < count:
            fetch(j + 4)

    total = jnp.zeros((3, rows, owned), jnp.bfloat16)
    for offset, blocks in zip(offsets, landed):
        for step, piece in enumerate(blocks):
            begin = (row ^ step) * quarter + offset
            total = lax.dynamic_update_slice(total, piece, (0, 0, begin))
    return total


def solution(mesh):
    in_specs = (
        P(None, ("col", "depth")),
        P("col", "depth"),
        P(("col", "depth")),
        P(("col", "depth")),
        P(),
        P(),
    )
    out_specs = P(None, "row", ("col", "depth"))
    return jax.shard_map(
        on_device, mesh=mesh, in_specs=in_specs, out_specs=out_specs, check_vma=False
    )
```

time: 625 us -> 562 us (0.90)
  waiting for transfers between devices: 378 us -> 304 us
  matrix products: 82.8 us -> 93.8 us
    ppermute x30, waiting for transfers between devices: 341 us -> 234 us  [the longest x15 205 us: fetch(): lax.ppermute(pieces[step], 'depth', [(i, (i + step) % n_depth) for i in r...]
    all_gather x1, waiting for transfers between devices: 37.3 us -> 69.9 us  [gather_panel(): block = lax.all_gather(block, ('col', 'depth'), axis=1, tiled=True)]
    dot_general x5, matrix products: 82.8 us -> 93.8 us  [multiply(): lax.dot_general(scaled, columns, (((1,), (1,)), ((), ())), preferred_elem...]
    dynamic_slice x2 -> x4, local copies, waits for them, and re-layouts: 12.2 us -> 16.9 us  [fetch(): lax.dynamic_slice(right_vectors, (begin + offsets[j], 0), (widths[j], gro...]
  transfers between devices with their start and end apart: 32 -> 32, of which waited for: 15 -> 12; matrix products, arithmetic and copies ran while one was open for 27% -> 36% of each run, Pallas kernels for 0% -> 0%
where the time goes in v2:
time: 562 us; the launch traced here: 558 us
  waiting for transfers between devices  304 us (54%)
  matrix products  93.8 us (17%)
  local copies, waits for them, and re-layouts  77.6 us (14%)
  other arithmetic  34.6 us (6%)
  starting transfers between devices  33.8 us (6%)
  between operations  14.5 us (3%)
    ppermute x15, waiting for transfers between devices, fetch(): lax.ppermute(pieces[step], 'depth', [(i, (i + step) % n_depth) for i in r...  205 us
    dot_general x5, matrix products, multiply(): lax.dot_general(scaled, columns, (((1,), (1,)), ((), ())), preferred_elem...  93.8 us
    all_gather x1, waiting for transfers between devices, gather_panel(): block = lax.all_gather(block, ('col', 'depth'), axis=1, tiled=True)  69.9 us
    ppermute x15, waiting for transfers between devices, multiply(): piece = lax.ppermute(piece, 'row', [(i, i ^ step) for i in range(n_row)])  28.8 us
    dynamic_update_slice x20, local copies, waits for them, and re-layouts, on_device(): total = lax.dynamic_update_slice(total, piece, (0, 0, begin))  25.9 us
    gather x2, local copies, waits for them, and re-layouts, gather_panel(): block = jnp.take(block, members, axis=1)  19 us
    ppermute x15, starting transfers between devices, fetch(): lax.ppermute(pieces[step], 'depth', [(i, (i + step) % n_depth) for i in r...  18.8 us
    convert_element_type x1, other arithmetic, gather_panel(): return scaled.astype(jnp.bfloat16).reshape(3 * P_SIZE, members.shape[0])  18.7 us
  transfers between devices with their start and end apart: 32, of which 12 were waited for; matrix products, arithmetic and copies ran while one was open for 36% of the time, Pallas kernels for 0%

profile of v2, /device:TPU:17, one launch (start us, length us, event | category | flops | bytes accessed | tf_op | source)
XLA Modules:
  0.0 557.8 jit_solution(15909772045945272703)
XLA Ops:
  15.8 11.0 %collective-permute-done.1 = bf16[128,1024]{1,0:T(8,128)(2,1)S(1)} collective-permute-done((bf16[128,1024]{1,0:T(8,128)(2,1)S(1)}, bf16[128,1024]{1,0:T(8,128)(2,1)S(1)}, u32[]{:S(2)}, u32[]{:S(2)}) %collective-permute-start.1) | collective-permute-done | bytes 262176 | tf_op jit(solution)/shard_map/ppermute | solution.py:82
  26.9 5.6 %collective-permute-done.2 = bf16[128,1024]{1,0:T(8,128)(2,1)S(1)} collective-permute-done((bf16[128,1024]{1,0:T(8,128)(2,1)S(1)}, bf16[128,1024]{1,0:T(8,128)(2,1)S(1)}, u32[]{:S(2)}, u32[]{:S(2)}) %collective-permute-start.2) | collective-permute-done | bytes 262176 | tf_op jit(solution)/shard_map/ppermute | solution.py:82
  32.6 5.5 constant_dynamic-slice_fusion
  42.3 69.9 %all-gather.4.cloned.1.call-done = bf16[272,4096]{0,1:T(8,128)(2,1)} async-done(((bf16[272,512]{0,1:T(8,128)(2,1)}), bf16[272,4096]{0,1:T(8,128)(2,1)}) %all-gather.4.cloned.1.call-update) | async-done | bytes 2228240 | tf_op jit(solution)/shard_map/all_gather | solution.py:35
  112.3 16.3 %gather_fusion.1 = bf16[4096,272]{1,0:T(8,128)(2,1)S(1)} fusion(bf16[272,4096]{0,1:T(8,128)(2,1)} %all-gather.4.cloned.1.call-done, s32[4096]{0:T(1024)S(1)} %broadcast_clamp_fusion), kind=kCustom, calls=%fused_computation.1 | custom fusion | bytes 4472832 | tf_op jit(solution)/shard_map/jit(_take)/gather | solution.py:36
  134.6 4.6 constant_dynamic-slice_fusion.8
  145.8 4.8 constant_dynamic-slice_fusion.4
  151.7 19.1 %collective-permute-done.6 = bf16[640,1024]{1,0:T(8,128)(2,1)} collective-permute-done((bf16[640,1024]{1,0:T(8,128)(2,1)}, bf16[640,1024]{1,0:T(8,128)(2,1)}, u32[]{:S(2)}, u32[]{:S(2)}) %collective-permute-start.6) | collective-permute-done | bytes 1310752 | tf_op jit(solution)/shard_map/ppermute | solution.py:82
  173.0 54.9 %collective-permute-done.7 = bf16[640,1024]{1,0:T(8,128)(2,1)} collective-permute-done((bf16[640,1024]{1,0:T(8,128)(2,1)}, bf16[640,1024]{1,0:T(8,128)(2,1)}, u32[]{:S(2)}, u32[]{:S(2)}) %collective-permute-start.7) | collective-permute-done | bytes 1310752 | tf_op jit(solution)/shard_map/ppermute | solution.py:82
  227.9 72.9 %collective-permute-done.8 = bf16[640,1024]{1,0:T(8,128)(2,1)} collective-permute-done((bf16[640,1024]{1,0:T(8,128)(2,1)S(1)}, bf16[640,1024]{1,0:T(8,128)(2,1)}, u32[]{:S(2)}, u32[]{:S(2)}) %collective-permute-start.8) | collective-permute-done | bytes 1310752 | tf_op jit(solution)/shard_map/ppermute | solution.py:82
  301.0 11.4 %convert_element_type.54 = f32[4,256,4096]{2,1,0:T(8,128)} convert(bf16[4,256,4096]{2,1,0:T(8,128)(2,1)} %bitcast.76) | non-fusion elementwise | flops 4194304 | bytes 25165824 | tf_op jit(solution)/shard_map/convert_element_type | solution.py:47
  312.4 18.7 %multiply_convert_fusion = bf16[4,3,256,4096]{3,2,1,0:T(8,128)(2,1)} fusion(f32[3,4096]{1,0:T(4,128)S(1)} %pad_maximum_fusion, f32[4,256,4096]{2,1,0:T(8,128)} %convert_element_type.54), kind=kLoop, calls=%fused_computation.2 | loop fusion | flops 25165824 | bytes 41992192 | tf_op jit(solution)/shard_map/convert_element_type | solution.py:48
  331.2 11.9 %convolution_convert_fusion.3 = bf16[3072,128]{1,0:T(8,128)(2,1)S(1)} fusion(bf16[3072,4096]{1,0:T(8,128)(2,1)} %bitcast.71, bf16[128,1024]{1,0:T(8,128)(2,1)S(1)} %copy-done.19, bf16[128,1024]{1,0:T(8,128)(2,1)S(1)} %copy-done.17, bf16[128,1024]{1,0:T(8,128)(2,1)S(1)} %copy-done.15, bf16[128,1024]{1,0:T(8,128)(2,1)S(1)} %copy-done.8), kind=kOutput, calls=%fused_computation.22 | convolution fusion | flops 3225812992 | bytes 27000832 | tf_op jit(solution)/shard_map/dot_general | solution.py:94
  343.8 17.7 %convolution_convert_fusion.2 = bf16[3072,384]{1,0:T(8,128)(2,1)S(1)} fusion(bf16[3072,4096]{1,0:T(8,128)(2,1)} %bitcast.72, bf16[384,1024]{1,0:T(8,128)(2,1)} %collective-permute-done.5, bf16[384,1024]{1,0:T(8,128)(2,1)} %collective-permute-done.4, bf16[384,1024]{1,0:T(8,128)(2,1)} %collective-permute-done.3, bf16[384,1024]{1,0:T(8,128)(2,1)S(1)} %copy-done.6), kind=kOutput, calls=%fused_computation.14 | convolution fusion | flops 9677438976 | bytes 30670848 | tf_op jit(solution)/shard_map/dot_general | solution.py:94
  361.5 25.7 %fusion.8 = bf16[3072,640]{1,0:T(8,128)(2,1)} fusion(bf16[3072,4096]{1,0:T(8,128)(2,1)} %bitcast.73, bf16[640,1024]{1,0:T(8,128)(2,1)} %collective-permute-done.8, bf16[640,1024]{1,0:T(8,128)(2,1)} %collective-permute-done.7, bf16[640,1024]{1,0:T(8,128)(2,1)} %collective-permute-done.6, bf16[640,1024]{1,0:T(8,128)(2,1)S(1)} %copy-done.1), kind=kOutput, calls=%fused_computation.11 | convolution fusion | flops 16129064960 | bytes 34340864 | tf_op jit(solution)/shard_map/dot_general | solution.py:94
  391.5 20.4 %convolution_convert_fusion = bf16[3072,512]{1,0:T(8,128)(2,1)} fusion(bf16[3072,4096]{1,0:T(8,128)(2,1)} %bitcast.74, bf16[512,1024]{1,0:T(8,128)(2,1)} %collective-permute-done.20, bf16[512,1024]{1,0:T(8,128)(2,1)} %collective-permute-done.19, bf16[512,1024]{1,0:T(8,128)(2,1)} %collective-permute-done.18, bf16[512,1024]{1,0:T(8,128)(2,1)} %get-tuple-element.57), kind=kOutput, calls=%fused_computation.12 | convolution fusion | flops 12903251968 | bytes 32505856 | tf_op jit(solution)/shard_map/dot_general | solution.py:94
  414.2 3.2 dynamic-slice_bitcast_fusion.4
  418.1 6.3 %broadcast_in_dim.25 = bf16[3,256,8192]{2,1,0:T(8,128)(2,1)} broadcast(bf16[]{:T(256)} %constant.137.clone.1), dimensions={} | broadcast | bytes 12582914 | tf_op jit(solution)/shard_map/broadcast_in_dim | solution.py:118
  426.3 3.4 collective-permute-done.11
  446.4 25.1 %collective-permute-done.25 = bf16[384,1024]{1,0:T(8,128)(2,1)S(1)} collective-permute-done((bf16[384,1024]{1,0:T(8,128)(2,1)}, bf16[384,1024]{1,0:T(8,128)(2,1)S(1)}, u32[]{:S(2)}, u32[]{:S(2)}) %collective-permute-start.25) | collective-permute-done | bytes 786464 | tf_op jit(solution)/shard_map/ppermute | solution.py:82
  472.7 15.6 %collective-permute-done.26 = bf16[384,1024]{1,0:T(8,128)(2,1)S(1)} collective-permute-done((bf16[384,1024]{1,0:T(8,128)(2,1)}, bf16[384,1024]{1,0:T(8,128)(2,1)S(1)}, u32[]{:S(2)}, u32[]{:S(2)}) %collective-permute-start.26) | collective-permute-done | bytes 786464 | tf_op jit(solution)/shard_map/ppermute | solution.py:82
  491.7 18.2 %convolution_convert_fusion.1 = bf16[3072,384]{1,0:T(8,128)(2,1)S(1)} fusion(bf16[3072,4096]{1,0:T(8,128)(2,1)} %bitcast.75, bf16[384,1024]{1,0:T(8,128)(2,1)} %copy-done.13, bf16[384,1024]{1,0:T(8,128)(2,1)} %copy-done.12, bf16[384,1024]{1,0:T(8,128)(2,1)} %collective-permute-done.24, bf16[384,1024]{1,0:T(8,128)(2,1)} %get-tuple-element.71), kind=kOutput, calls=%fused_computation.13 | convolution fusion | flops 9677438976 | bytes 30670848 | tf_op jit(solution)/shard_map/dot_general | solution.py:94
  520.2 3.8 collective-permute-done.22
  527.6 21.7 %collective-permute-done.28 = bf16[3,256,384]{2,1,0:T(8,128)(2,1)S(1)} collective-permute-done((bf16[3,256,384]{2,1,0:T(8,128)(2,1)S(1)}, bf16[3,256,384]{2,1,0:T(8,128)(2,1)S(1)}, u32[]{:S(2)}, u32[]{:S(2)}) %collective-permute-start.28) | collective-permute-done | bytes 589856 | tf_op jit(solution)/shard_map/ppermute | solution.py:103
  (147 shorter events, 75.5 us)
Async XLA Ops:
  6.5 105.7 %all-gather.4.cloned.1.call-start = ((), (), s32[]{:S(2)}) async-start(), calls=%async_computation | async-start | bytes 3538944 | tf_op jit(solution)/shard_map/all_gather | solution.py:35
  32.5 268.5 %all-gather.6.cloned.1.call-start = ((), (), s32[]{:S(2)}) async-start(), calls=%async_computation.1 | async-start | bytes 10485760 | tf_op jit(solution)/shard_map/all_gather | solution.py:43
  38.1 96.4 %collective-permute-start.3 = (bf16[384,1024]{1,0:T(8,128)(2,1)}, bf16[384,1024]{1,0:T(8,128)(2,1)}, u32[]{:S(2)}, u32[]{:S(2)}) collective-permute-start(bf16[384,1024]{1,0:T(8,128)(2,1)} %get-tuple-element.90), channel_id=1, source_target_pairs={{0,1},{1,2},{2,3},{3,0},{4,5},{5,6},{6,7},{7,4},{8,9},{9,10},{10,1... | collective-permute-start | bytes 2359304 | tf_op jit(solution)/shard_map/ppermute | solution.py:82
  39.4 95.1 %collective-permute-start.4 = (bf16[384,1024]{1,0:T(8,128)(2,1)}, bf16[384,1024]{1,0:T(8,128)(2,1)}, u32[]{:S(2)}, u32[]{:S(2)}) collective-permute-start(bf16[384,1024]{1,0:T(8,128)(2,1)} %get-tuple-element.89), channel_id=1, source_target_pairs={{0,2},{1,3},{2,0},{3,1},{4,6},{5,7},{6,4},{7,5},{8,10},{9,11},{10,... | collective-permute-start | bytes 2359304 | tf_op jit(solution)/shard_map/ppermute | solution.py:82
  41.5 93.0 %collective-permute-start.5 = (bf16[384,1024]{1,0:T(8,128)(2,1)}, bf16[384,1024]{1,0:T(8,128)(2,1)}, u32[]{:S(2)}, u32[]{:S(2)}) collective-permute-start(bf16[384,1024]{1,0:T(8,128)(2,1)} %get-tuple-element.88), channel_id=1, source_target_pairs={{0,3},{1,0},{2,1},{3,2},{4,7},{5,4},{6,5},{7,6},{8,11},{9,8},{10,9... | collective-permute-start | bytes 2359304 | tf_op jit(solution)/shard_map/ppermute | solution.py:82
  139.3 31.6 %collective-permute-start.6 = (bf16[640,1024]{1,0:T(8,128)(2,1)}, bf16[640,1024]{1,0:T(8,128)(2,1)}, u32[]{:S(2)}, u32[]{:S(2)}) collective-permute-start(bf16[640,1024]{1,0:T(8,128)(2,1)} %get-tuple-element.42), channel_id=1, source_target_pairs={{0,1},{1,2},{2,3},{3,0},{4,5},{5,6},{6,7},{7,4},{8,9},{9,10},{10,1... | collective-permute-start | bytes 3932168 | tf_op jit(solution)/shard_map/ppermute | solution.py:82
  141.3 86.6 %collective-permute-start.7 = (bf16[640,1024]{1,0:T(8,128)(2,1)}, bf16[640,1024]{1,0:T(8,128)(2,1)}, u32[]{:S(2)}, u32[]{:S(2)}) collective-permute-start(bf16[640,1024]{1,0:T(8,128)(2,1)} %get-tuple-element.43), channel_id=1, source_target_pairs={{0,2},{1,3},{2,0},{3,1},{4,6},{5,7},{6,4},{7,5},{8,10},{9,11},{10,... | collective-permute-start | bytes 3932168 | tf_op jit(solution)/shard_map/ppermute | solution.py:82
  143.4 157.4 %collective-permute-start.8 = (bf16[640,1024]{1,0:T(8,128)(2,1)S(1)}, bf16[640,1024]{1,0:T(8,128)(2,1)}, u32[]{:S(2)}, u32[]{:S(2)}) collective-permute-start(bf16[640,1024]{1,0:T(8,128)(2,1)S(1)} %get-tuple-element.44), channel_id=1, source_target_pairs={{0,3},{1,0},{2,1},{3,2},{4,7},{5,4},{6,5},{7,6},{8,11},{9,8},{10,9... | collective-permute-start | bytes 3932168 | tf_op jit(solution)/shard_map/ppermute | solution.py:82
  150.5 238.0 %collective-permute-start.18 = (bf16[512,1024]{1,0:T(8,128)(2,1)}, bf16[512,1024]{1,0:T(8,128)(2,1)}, u32[]{:S(2)}, u32[]{:S(2)}) collective-permute-start(bf16[512,1024]{1,0:T(8,128)(2,1)} %get-tuple-element.54), channel_id=1, source_target_pairs={{0,1},{1,2},{2,3},{3,0},{4,5},{5,6},{6,7},{7,4},{8,9},{9,10},{10,1... | collective-permute-start | bytes 3145736 | tf_op jit(solution)/shard_map/ppermute | solution.py:82
  150.5 238.0 %collective-permute-start.19 = (bf16[512,1024]{1,0:T(8,128)(2,1)}, bf16[512,1024]{1,0:T(8,128)(2,1)}, u32[]{:S(2)}, u32[]{:S(2)}) collective-permute-start(bf16[512,1024]{1,0:T(8,128)(2,1)} %get-tuple-element.55), channel_id=1, source_target_pairs={{0,2},{1,3},{2,0},{3,1},{4,6},{5,7},{6,4},{7,5},{8,10},{9,11},{10,... | collective-permute-start | bytes 3145736 | tf_op jit(solution)/shard_map/ppermute | solution.py:82
  170.8 217.7 %collective-permute-start.20 = (bf16[512,1024]{1,0:T(8,128)(2,1)}, bf16[512,1024]{1,0:T(8,128)(2,1)}, u32[]{:S(2)}, u32[]{:S(2)}) collective-permute-start(bf16[512,1024]{1,0:T(8,128)(2,1)} %get-tuple-element.56), channel_id=1, source_target_pairs={{0,3},{1,0},{2,1},{3,2},{4,7},{5,4},{6,5},{7,6},{8,11},{9,8},{10,9... | collective-permute-start | bytes 3145736 | tf_op jit(solution)/shard_map/ppermute | solution.py:82
  343.1 94.0 %collective-permute-start.24 = (bf16[384,1024]{1,0:T(8,128)(2,1)}, bf16[384,1024]{1,0:T(8,128)(2,1)}, u32[]{:S(2)}, u32[]{:S(2)}) collective-permute-start(bf16[384,1024]{1,0:T(8,128)(2,1)} %get-tuple-element.64), channel_id=1, source_target_pairs={{0,1},{1,2},{2,3},{3,0},{4,5},{5,6},{6,7},{7,4},{8,9},{9,10},{10,1... | collective-permute-start | bytes 2359304 | tf_op jit(solution)/shard_map/ppermute | solution.py:82
  391.1 39.8 %collective-permute-start.12 = (bf16[3,256,384]{2,1,0:T(8,128)(2,1)}, bf16[3,256,384]{2,1,0:T(8,128)(2,1)}, u32[]{:S(2)}, u32[]{:S(2)}) collective-permute-start(bf16[3,256,384]{2,1,0:T(8,128)(2,1)} %get-tuple-element.115), channel_id=1, source_target_pairs={{0,8},{8,0},{16,24},{24,16},{1,9},{9,1},{17,25},{25,17},{2,10},{10... | collective-permute-start | bytes 1769480 | tf_op jit(solution)/shard_map/ppermute | solution.py:103
  391.3 40.9 %collective-permute-start.13 = (bf16[3,256,384]{2,1,0:T(8,128)(2,1)}, bf16[3,256,384]{2,1,0:T(8,128)(2,1)}, u32[]{:S(2)}, u32[]{:S(2)}) collective-permute-start(bf16[3,256,384]{2,1,0:T(8,128)(2,1)} %get-tuple-element.114), channel_id=1, source_target_pairs={{0,16},{8,24},{16,0},{24,8},{1,17},{9,25},{17,1},{25,9},{2,18},{10... | collective-permute-start | bytes 1769480 | tf_op jit(solution)/shard_map/ppermute | solution.py:103
  429.7 59.9 %collective-permute-start.15 = (bf16[3,256,640]{2,1,0:T(8,128)(2,1)S(1)}, bf16[3,256,640]{2,1,0:T(8,128)(2,1)S(1)}, u32[]{:S(2)}, u32[]{:S(2)}) collective-permute-start(bf16[3,256,640]{2,1,0:T(8,128)(2,1)S(1)} %get-tuple-element.106), channel_id=1, source_target_pairs={{0,8},{8,0},{16,24},{24,16},{1,9},{9,1},{17,25},{25,17},{2,10},{10... | collective-permute-start | bytes 2949128 | tf_op jit(solution)/shard_map/ppermute | solution.py:103
  430.9 59.8 %collective-permute-start.16 = (bf16[3,256,640]{2,1,0:T(8,128)(2,1)S(1)}, bf16[3,256,640]{2,1,0:T(8,128)(2,1)S(1)}, u32[]{:S(2)}, u32[]{:S(2)}) collective-permute-start(bf16[3,256,640]{2,1,0:T(8,128)(2,1)S(1)} %get-tuple-element.105), channel_id=1, source_target_pairs={{0,16},{8,24},{16,0},{24,8},{1,17},{9,25},{17,1},{25,9},{2,18},{10... | collective-permute-start | bytes 2949128 | tf_op jit(solution)/shard_map/ppermute | solution.py:103
  432.2 59.5 %collective-permute-start.17 = (bf16[3,256,640]{2,1,0:T(8,128)(2,1)S(1)}, bf16[3,256,640]{2,1,0:T(8,128)(2,1)}, u32[]{:S(2)}, u32[]{:S(2)}) collective-permute-start(bf16[3,256,640]{2,1,0:T(8,128)(2,1)S(1)} %get-tuple-element.104), channel_id=1, source_target_pairs={{0,24},{8,16},{16,8},{24,0},{1,25},{9,17},{17,9},{25,1},{2,26},{10... | collective-permute-start | bytes 2949128 | tf_op jit(solution)/shard_map/ppermute | solution.py:103
  434.6 36.8 %collective-permute-start.25 = (bf16[384,1024]{1,0:T(8,128)(2,1)}, bf16[384,1024]{1,0:T(8,128)(2,1)S(1)}, u32[]{:S(2)}, u32[]{:S(2)}) collective-permute-start(bf16[384,1024]{1,0:T(8,128)(2,1)} %get-tuple-element.65), channel_id=1, source_target_pairs={{0,2},{1,3},{2,0},{3,1},{4,6},{5,7},{6,4},{7,5},{8,10},{9,11},{10,... | collective-permute-start | bytes 2359304 | tf_op jit(solution)/shard_map/ppermute | solution.py:82
  437.0 51.2 %collective-permute-start.26 = (bf16[384,1024]{1,0:T(8,128)(2,1)}, bf16[384,1024]{1,0:T(8,128)(2,1)S(1)}, u32[]{:S(2)}, u32[]{:S(2)}) collective-permute-start(bf16[384,1024]{1,0:T(8,128)(2,1)} %get-tuple-element.66), channel_id=1, source_target_pairs={{0,3},{1,0},{2,1},{3,2},{4,7},{5,4},{6,5},{7,6},{8,11},{9,8},{10,9... | collective-permute-start | bytes 2359304 | tf_op jit(solution)/shard_map/ppermute | solution.py:82
  471.4 46.6 %collective-permute-start.21 = (bf16[3,256,512]{2,1,0:T(8,128)(2,1)}, bf16[3,256,512]{2,1,0:T(8,128)(2,1)S(1)}, u32[]{:S(2)}, u32[]{:S(2)}) collective-permute-start(bf16[3,256,512]{2,1,0:T(8,128)(2,1)} %get-tuple-element.109), channel_id=1, source_target_pairs={{0,8},{8,0},{16,24},{24,16},{1,9},{9,1},{17,25},{25,17},{2,10},{10... | collective-permute-start | bytes 2359304 | tf_op jit(solution)/shard_map/ppermute | solution.py:103
  488.3 35.6 %collective-permute-start.22 = (bf16[3,256,512]{2,1,0:T(8,128)(2,1)}, bf16[3,256,512]{2,1,0:T(8,128)(2,1)S(1)}, u32[]{:S(2)}, u32[]{:S(2)}) collective-permute-start(bf16[3,256,512]{2,1,0:T(8,128)(2,1)} %get-tuple-element.108), channel_id=1, source_target_pairs={{0,16},{8,24},{16,0},{24,8},{1,17},{9,25},{17,1},{25,9},{2,18},{10... | collective-permute-start | bytes 2359304 | tf_op jit(solution)/shard_map/ppermute | solution.py:103
  489.5 35.3 %collective-permute-start.23 = (bf16[3,256,512]{2,1,0:T(8,128)(2,1)}, bf16[3,256,512]{2,1,0:T(8,128)(2,1)S(1)}, u32[]{:S(2)}, u32[]{:S(2)}) collective-permute-start(bf16[3,256,512]{2,1,0:T(8,128)(2,1)} %get-tuple-element.107), channel_id=1, source_target_pairs={{0,24},{8,16},{16,8},{24,0},{1,25},{9,17},{17,9},{25,1},{2,26},{10... | collective-permute-start | bytes 2359304 | tf_op jit(solution)/shard_map/ppermute | solution.py:103
  511.2 38.0 %collective-permute-start.28 = (bf16[3,256,384]{2,1,0:T(8,128)(2,1)S(1)}, bf16[3,256,384]{2,1,0:T(8,128)(2,1)S(1)}, u32[]{:S(2)}, u32[]{:S(2)}) collective-permute-start(bf16[3,256,384]{2,1,0:T(8,128)(2,1)S(1)} %get-tuple-element.111), channel_id=1, source_target_pairs={{0,16},{8,24},{16,0},{24,8},{1,17},{9,25},{17,1},{25,9},{2,18},{10... | collective-permute-start | bytes 1769480 | tf_op jit(solution)/shard_map/ppermute | solution.py:103
  518.0 32.1 %collective-permute-start.29 = (bf16[3,256,384]{2,1,0:T(8,128)(2,1)S(1)}, bf16[3,256,384]{2,1,0:T(8,128)(2,1)S(1)}, u32[]{:S(2)}, u32[]{:S(2)}) collective-permute-start(bf16[3,256,384]{2,1,0:T(8,128)(2,1)S(1)} %get-tuple-element.110), channel_id=1, source_target_pairs={{0,24},{8,16},{16,8},{24,0},{1,25},{9,17},{17,9},{25,1},{2,26},{10... | collective-permute-start | bytes 1769480 | tf_op jit(solution)/shard_map/ppermute | solution.py:103
  (28 other events, 479.4 us)
Sparse Core Ops, SparseCore 0:
  32.6 79.5 all-gather.3
  134.7 89.3 all-gather.5
